TPU v7x, 256 devices: a whole 4x4x8 slice. The times are simulated.
256 devices in a mesh: seq: 32 (over z_hi, x, core), tp: 8 (over y, z_lo).
Axes of the slice: x: 4, y: 4, z: 8 (z_hi: 4, z_lo: 2; z = z_hi * 2 + z_lo), core: 2. Of those that a mesh axis runs over, the one named last changes fastest.
Arguments:
- frame_grid: bfloat16 [64, 256, 8, 6, 128], P('seq', None, 'tp'), may hold values from -8 to 8
- keep_rows: int32 [64, 256], P('seq'), may hold values from 0 to 255, as said below
- kept_count: int32 [64], replicated, may hold values from 36 to 220, as said below
- frame_slot: int32 [64], replicated, may hold values from 0 to 63, as said below
- out_weight: bfloat16 [4096, 8192], P('tp'), may hold values from -0.125 to 0.125
- residual: bfloat16 [8192, 8192], P('seq', 'tp'), may hold values from -48 to 48
- norm_gain: bfloat16 [8192], P('tp'), may hold values from 0.5 to 1.5
Outputs:
- hidden: bfloat16 [8192, 8192], P('seq', 'tp')
- normed: bfloat16 [8192, 8192], P('seq', 'tp')
Inputs may be any that keep to these rules, and one draw needn't show every extreme that they name: `kept_count`: frames follow one another in the sequence in the order of f; the counts sum to 8192. `frame_slot`: each slot holds exactly one frame. `keep_rows`: in the slot of frame f the first kept_count[f] entries are distinct grid rows in ascending order; the other entries are the remaining rows.
All inputs are finite; a program needn't handle non-finite values.
Results may differ from a plain program's by a relative error of at most 0.009.
Values may be sent and summed in bfloat16 or wider, within the bound.
A program may use at most 192 MiB of HBM per device.

v0:
```python
import functools
import math

import jax
import jax.numpy as jnp
import numpy as np
from jax import lax
from jax.experimental import pallas as pl
from jax.experimental.pallas import tpu as pltpu
from jax.sharding import PartitionSpec as P

D = 8192
HD = 128
HEADS = 4
FRAMES = 64
GRID = 256
TOK = 256
N_SEQ = 32
N_TP = 8
WIDTH = D // N_TP
PAIR = 16
CHUNKS = 4
ROWS = TOK // CHUNKS
KEY_AT = (0, 80, 144, 208, 256)
KEY_ROWS = tuple(KEY_AT[i + 1] - KEY_AT[i] for i in range(CHUNKS))
KEY_BLOCK = 1024
NEGATIVE = -1e30
EPSILON = 1e-06
SCALE = 1.0 / math.sqrt(HD)
MESH = pl.DeviceIdType.MESH
F32 = jnp.float32
BF16 = jnp.bfloat16


def key_positions():
    out = []
    for chunk in range(CHUNKS):
        x, c, z, l = np.meshgrid(
            np.arange(4), np.arange(2), np.arange(4), np.arange(KEY_AT[chunk], KEY_AT[chunk + 1]), indexing="ij"
        )
        out.append((l * N_SEQ + (z * 4 + x) * 2 + c).reshape(-1))
    return np.concatenate(out).astype(np.int32)[None, :]


def iota(shape, dim):
    return lax.broadcasted_iota(jnp.int32, shape, dim)


def one_hot(mask):
    return jnp.where(mask, 1.0, 0.0).astype(BF16)


def dot(a, b, contract):
    return lax.dot_general(a, b, ((contract[:1], contract[1:]), ((), ())), preferred_element_type=F32)


def kernel(
    x_ref, keep_ref, count_ref, slot_ref, kpos_ref, w_hbm, res_ref, gain_ref,
    hid_ref, nrm_ref,
    send_kv, send_q, recv_kv, recv_q, kv0, kv1, kv2, kv3, q_ref, w_ref,
    m_ref, den_ref, acc_ref, att_ref, part_ref, half_p, half_m, block_p, block_m,
    z_send, z_recv, stream_ref, ssq_ref, ssq_send, ssq_recv,
    a2a_sem, g_send, g_recv, r_send, r_recv, s_sem, w_sem,
):
    kvs = (kv0, kv1, kv2, kv3)
    me = lax.axis_index("seq")
    tp = lax.axis_index("tp")
    zz, xx, cc = me >> 3, (me >> 1) & 3, me & 1
    yy, zl = tp >> 1, tp & 1

    def seq_id(z, x, c):
        return {"seq": (((z & 3) * 4 + (x & 3)) * 2 + c)}

    def tp_id(y, z):
        return {"tp": (y & 3) * 2 + z}

    w_copy = pltpu.make_async_copy(w_hbm, w_ref, w_sem)
    w_copy.start()

    barrier = pltpu.get_barrier_semaphore()

    @pl.loop(1, N_SEQ)
    def _(o):
        pl.semaphore_signal(barrier, inc=1, device_id={"seq": (me + o) & 31}, device_id_type=MESH)

    @pl.loop(1, N_TP)
    def _(o):
        pl.semaphore_signal(barrier, inc=1, device_id={"tp": (tp + o) & 7}, device_id_type=MESH)

    f_col, f_row = iota((FRAMES, FRAMES), 0), iota((FRAMES, FRAMES), 1)
    counts, slots = count_ref[...], slot_ref[...]
    starts_col = jnp.sum(jnp.where(f_row < f_col, counts, 0), axis=1, keepdims=True)
    count_col = jnp.sum(jnp.where(f_row == f_col, counts, 0), axis=1, keepdims=True)
    slot_col = jnp.sum(jnp.where(f_row == f_col, slots, 0), axis=1, keepdims=True)
    ends_row = jnp.sum(jnp.where(f_col <= f_row, count_col, 0), axis=0, keepdims=True)

    r_id = iota((N_SEQ * PAIR, 1), 0)
    second = ((r_id >> 3) & 1) == 1

    def own(fl, values):
        return jnp.sum(jnp.where(slot_col == 2 * me + fl, values, 0), axis=0, keepdims=True)

    first_r = jnp.where(second, own(1, starts_col), own(0, starts_col))
    count_r = jnp.where(second, own(1, count_col), own(0, count_col))
    offset_r = (((r_id >> 4) - first_r) & 31) + 32 * (r_id & 7)
    offset_r = jnp.where(offset_r < count_r, offset_r, -1)
    picked = []
    for fl in range(2):
        wanted = jnp.where(second if fl else jnp.logical_not(second), offset_r, -1)
        chosen = one_hot(iota((N_SEQ * PAIR, GRID), 1) == wanted)
        kept = one_hot(iota((GRID, GRID), 0) == keep_ref[fl : fl + 1, :])
        picked.append(dot(chosen, kept, (1, 1)).astype(BF16))
    pick = jnp.concatenate(picked, axis=1)
    send_kv[...] = dot(pick, x_ref[:, HEADS * HD :], (1, 0)).astype(BF16).reshape(N_SEQ, PAIR, 2 * HD)

    pl.semaphore_wait(barrier, N_SEQ - 1 + N_TP - 1)

    def exchange(src, dst, at):
        @pl.loop(1, N_SEQ)
        def _(o):
            other = (me + o) & 31
            pltpu.make_async_remote_copy(
                src_ref=src.at[other],
                dst_ref=dst.at[me],
                send_sem=a2a_sem.at[at],
                recv_sem=a2a_sem.at[at + 1],
                device_id={"seq": other},
                device_id_type=MESH,
            ).start()

    def exchange_all(src, dst, at):
        return pltpu.make_async_remote_copy(
            src_ref=src.at[pl.ds(0, N_SEQ - 1)],
            dst_ref=dst.at[pl.ds(0, N_SEQ - 1)],
            send_sem=a2a_sem.at[at],
            recv_sem=a2a_sem.at[at + 1],
            device_id={"seq": (me + 1) & 31},
            device_id_type=MESH,
        )

    exchange(send_kv, recv_kv, 0)
    recv_kv[pl.ds(me, 1)] = send_kv[pl.ds(me, 1)]
    send_q[...] = dot(pick, x_ref[:, : HEADS * HD], (1, 0)).astype(BF16).reshape(N_SEQ, PAIR, HEADS * HD)

    lane = iota((1, N_SEQ * PAIR), 1)
    at_slot = slot_col == (iota((FRAMES, N_SEQ * PAIR), 1) >> 3)
    first_l = jnp.sum(jnp.where(at_slot, starts_col, 0), axis=0, keepdims=True)
    count_l = jnp.sum(jnp.where(at_slot, count_col, 0), axis=0, keepdims=True)
    offset_l = ((me - first_l) & 31) + 32 * (lane & 7)
    row_l = jnp.where(offset_l < count_l, (first_l + offset_l) >> 5, -1)
    place = one_hot(iota((TOK, N_SEQ * PAIR), 0) == row_l)
    q_pos = iota((TOK, 1), 0) * N_SEQ + me
    ends = jnp.min(jnp.where(ends_row > q_pos, ends_row, 2 * D), axis=1, keepdims=True)

    kv_all = exchange_all(send_kv, recv_kv, 0)
    kv_all.wait_recv()
    mine = dot(place, recv_kv[...].reshape(N_SEQ * PAIR, 2 * HD), (1, 0)).astype(BF16)
    for c in range(CHUNKS):
        kvs[c][xx, cc, zz] = mine[KEY_AT[c] : KEY_AT[c + 1], :]

    def seq_copy(c, at, src, dst, device):
        return pltpu.make_async_remote_copy(
            src_ref=src, dst_ref=dst, send_sem=g_send.at[c, at], recv_sem=g_recv.at[c, at],
            device_id=device, device_id_type=MESH,
        )

    def z_one(c):
        ref = kvs[c].at[xx, cc, zz]
        return [
            seq_copy(c, 0, ref, ref, seq_id(zz + 1, xx, cc)),
            seq_copy(c, 1, ref, ref, seq_id(zz - 1, xx, cc)),
        ]

    def z_two(c):
        cut = KEY_ROWS[c] // 32 * 16
        up = kvs[c].at[xx, cc, (zz - 1) & 3, pl.ds(0, cut)]
        down = kvs[c].at[xx, cc, (zz + 1) & 3, pl.ds(cut, KEY_ROWS[c] - cut)]
        return [
            seq_copy(c, 2, up, up, seq_id(zz + 1, xx, cc)),
            seq_copy(c, 3, down, down, seq_id(zz - 1, xx, cc)),
        ]

    def x_one(c):
        ref = kvs[c].at[xx, cc]
        return [
            seq_copy(c, 4, ref, ref, seq_id(zz, xx + 1, cc)),
            seq_copy(c, 5, ref, ref, seq_id(zz, xx - 1, cc)),
        ]

    def x_two(c):
        up = kvs[c].at[(xx - 1) & 3, cc, pl.ds(0, 2)]
        down = kvs[c].at[(xx + 1) & 3, cc, pl.ds(2, 2)]
        return [
            seq_copy(c, 6, up, up, seq_id(zz, xx + 1, cc)),
            seq_copy(c, 7, down, down, seq_id(zz, xx - 1, cc)),
        ]

    def sibling(c, step):
        ref = kvs[c].at[(xx + step) & 3, cc]
        return [seq_copy(c, 8 + step, ref, ref, seq_id(zz, xx, 1 - cc))]

    def start(copies):
        for copy in copies:
            copy.start()

    def wait_recv(copies):
        for copy in copies:
            copy.wait_recv()

    def wait_send(copies):
        for copy in copies:
            copy.wait_send()

    def gather_stage(stage, c):
        if stage == 1:
            wait_recv(z_one(c))
            start(z_two(c))
        elif stage == 2:
            wait_recv(z_two(c))
            start(x_one(c))
            start(sibling(c, 0))
        elif stage == 3:
            wait_recv(x_one(c))
            start(x_two(c))
            start(sibling(c, 1))
            start(sibling(c, 3))
        elif stage == 4:
            wait_recv(x_two(c))
            start(sibling(c, 2))
        elif stage == 5:
            for step in range(4):
                wait_recv(sibling(c, step))

    for c in range(CHUNKS):
        start(z_one(c))
    exchange(send_q, recv_q, 2)
    recv_q[pl.ds(me, 1)] = send_q[pl.ds(me, 1)]

    def load_queries():
        exchange_all(send_q, recv_q, 2).wait_recv()
        queries = dot(place, recv_q[...].reshape(N_SEQ * PAIR, HEADS * HD), (1, 0)).astype(BF16)
        for a in range(HEADS):
            q_ref[a] = queries[:, a * HD : (a + 1) * HD]

    def attention(j):
        q = q_ref[:, j * ROWS : (j + 1) * ROWS, :].reshape(HEADS * ROWS, HD)
        end = jnp.concatenate([ends[j * ROWS : (j + 1) * ROWS]] * HEADS, axis=0)
        m_ref[...] = jnp.full_like(m_ref, NEGATIVE)
        den_ref[...] = jnp.zeros_like(den_ref)
        acc_ref[...] = jnp.zeros_like(acc_ref)
        for c in range(j + 1):
            total = KEY_ROWS[c] * N_SEQ
            block = total // (total // KEY_BLOCK)
            flat = kvs[c].reshape(total, 2 * HD)

            @pl.loop(0, total // block)
            def _(i, c=c, block=block, flat=flat):
                at = pl.multiple_of(i * block, 128)
                keys = flat[pl.ds(at, block), :HD]
                values = flat[pl.ds(at, block), HD:]
                s = dot(q, keys, (1, 1))
                if c >= j - 1:
                    pos = kpos_ref[:, pl.ds(pl.multiple_of(KEY_AT[c] * N_SEQ + at, 128), block)]
                    s = jnp.where(pos < end, s, NEGATIVE)
                old = m_ref[:, :1]
                new = jnp.maximum(old, jnp.max(s, axis=1, keepdims=True))
                p = jnp.exp((s - new) * SCALE)
                keep = jnp.exp((old - new) * SCALE)
                m_ref[...] = jnp.broadcast_to(new, m_ref.shape)
                den_ref[...] = den_ref[...] * keep + jnp.sum(p, axis=1, keepdims=True)
                acc_ref[...] = acc_ref[...] * keep + dot(p.astype(BF16), values, (1, 0))

        out = (acc_ref[...] / den_ref[...]).astype(BF16)
        att_ref[...] = jnp.concatenate([out[a * ROWS : (a + 1) * ROWS] for a in range(HEADS)], axis=1)

    def tp_copy(j, at, src, dst, device):
        return pltpu.make_async_remote_copy(
            src_ref=src, dst_ref=dst, send_sem=r_send.at[j, at], recv_sem=r_recv.at[j, at],
            device_id=device, device_id_type=MESH,
        )

    y_up, y_down, y_far = (yy + 1) & 3, (yy - 1) & 3, (yy + 2) & 3

    def far_halves(j):
        return [
            tp_copy(j, 0, part_ref.at[j, 2 * y_far], half_p.at[j], tp_id(yy + 1, zl)),
            tp_copy(j, 1, part_ref.at[j, 2 * y_far + 1], half_m.at[j], tp_id(yy - 1, zl)),
        ]

    def near_blocks(j):
        return [
            tp_copy(j, 2, part_ref.at[j, pl.ds(2 * y_up, 2)], block_p.at[j], tp_id(yy + 1, zl)),
            tp_copy(j, 3, part_ref.at[j, pl.ds(2 * y_down, 2)], block_m.at[j], tp_id(yy - 1, zl)),
        ]

    def z_pair(j):
        return [tp_copy(j, 4, z_send.at[j], z_recv.at[j], tp_id(yy, 1 - zl))]

    def project(j):
        def columns(y):
            @pl.loop(0, 2)
            def _(h):
                t = 2 * y + h
                w = w_ref[:, pl.ds(pl.multiple_of(t * WIDTH, WIDTH), WIDTH)]
                part_ref[j, t] = dot(att_ref[...], w, (1, 0)).astype(BF16)

        columns(y_far)
        start(far_halves(j))
        columns(y_up)
        columns(y_down)
        columns(yy)

    def reduce_near(j):
        wait_recv(far_halves(j))
        part_ref[j, 2 * y_up] = (part_ref[j, 2 * y_up].astype(F32) + half_p[j].astype(F32)).astype(BF16)
        part_ref[j, 2 * y_down + 1] = (part_ref[j, 2 * y_down + 1].astype(F32) + half_m[j].astype(F32)).astype(BF16)
        start(near_blocks(j))

    def reduce_own(j):
        wait_recv(near_blocks(j))

        def total(h):
            return part_ref[j, 2 * yy + h].astype(F32) + block_p[j, h].astype(F32) + block_m[j, h].astype(F32)

        z_send[j] = total(1 - zl).astype(BF16)
        start(z_pair(j))
        rows = pl.ds(j * ROWS, ROWS)
        stream_ref[rows, :] = total(zl) + res_ref[rows, :].astype(F32)

    def finish_rows(j):
        wait_recv(z_pair(j))
        rows = pl.ds(j * ROWS, ROWS)
        stream = stream_ref[rows, :] + z_recv[j].astype(F32)
        stream_ref[rows, :] = stream
        hid_ref[rows, :] = stream.astype(BF16)
        ssq_ref[rows, :] = jnp.broadcast_to(jnp.sum(stream * stream, axis=1, keepdims=True), (ROWS, HD))

    gather_stage(1, 0)
    gather_stage(2, 0)
    gather_stage(1, 1)
    gather_stage(3, 0)
    gather_stage(2, 1)
    gather_stage(1, 2)
    gather_stage(4, 0)
    gather_stage(3, 1)
    gather_stage(2, 2)
    gather_stage(1, 3)
    load_queries()
    gather_stage(5, 0)
    gather_stage(4, 1)
    gather_stage(3, 2)
    gather_stage(2, 3)
    attention(0)
    w_copy.wait()
    project(0)
    gather_stage(5, 1)
    gather_stage(4, 2)
    gather_stage(3, 3)
    attention(1)
    reduce_near(0)
    project(1)
    gather_stage(5, 2)
    gather_stage(4, 3)
    attention(2)
    reduce_near(1)
    reduce_own(0)
    project(2)
    gather_stage(5, 3)
    attention(3)
    reduce_near(2)
    reduce_own(1)
    project(3)
    finish_rows(0)
    reduce_near(3)
    reduce_own(2)
    finish_rows(1)
    reduce_own(3)
    finish_rows(2)
    finish_rows(3)

    diag = iota((TOK, TOK), 0) == iota((TOK, TOK), 1)
    ssq_row = jnp.sum(jnp.where(diag, ssq_ref[:, :1], 0.0), axis=0, keepdims=True)
    ssq_send[...] = jnp.broadcast_to(ssq_row, (8, TOK))
    ssq_recv[pl.ds(tp, 1)] = ssq_send[...][None]

    @pl.loop(1, N_TP)
    def _(o):
        pltpu.make_async_remote_copy(
            src_ref=ssq_send, dst_ref=ssq_recv.at[tp], send_sem=s_sem.at[0], recv_sem=s_sem.at[1],
            device_id={"tp": (tp + o) & 7}, device_id_type=MESH,
        ).start()

    ssq_all = pltpu.make_async_remote_copy(
        src_ref=ssq_recv.at[pl.ds(0, N_TP - 1)], dst_ref=ssq_recv.at[pl.ds(0, N_TP - 1)],
        send_sem=s_sem.at[0], recv_sem=s_sem.at[1],
        device_id={"tp": (tp + 1) & 7}, device_id_type=MESH,
    )
    ssq_all.wait_recv()
    sums = jnp.sum(ssq_recv[...], axis=0)[:1, :]
    inverse_row = lax.rsqrt(sums / D + EPSILON)
    inverse = jnp.sum(jnp.where(diag, inverse_row, 0.0), axis=1, keepdims=True)
    nrm_ref[...] = (stream_ref[...] * inverse * gain_ref[...].astype(F32)).astype(BF16)

    ssq_all.wait_send()
    kv_all.wait_send()
    exchange_all(send_q, recv_q, 2).wait_send()
    for c in range(CHUNKS):
        wait_send(z_one(c) + z_two(c) + x_one(c) + x_two(c))
        for step in range(4):
            wait_send(sibling(c, step))
        wait_send(far_halves(c) + near_blocks(c) + z_pair(c))


def body(frame_grid, keep_rows, kept_count, frame_slot, out_weight, residual, norm_gain):
    vmem = pl.BlockSpec(memory_space=pltpu.VMEM)
    dma = pltpu.SemaphoreType.DMA
    return pl.pallas_call(
        kernel,
        out_shape=[jax.ShapeDtypeStruct((TOK, WIDTH), BF16)] * 2,
        in_specs=[vmem] * 5 + [pl.BlockSpec(memory_space=pl.ANY)] + [vmem] * 2,
        out_specs=[vmem] * 2,
        scratch_shapes=[
            pltpu.VMEM((N_SEQ, PAIR, 2 * HD), BF16),
            pltpu.VMEM((N_SEQ, PAIR, HEADS * HD), BF16),
            pltpu.VMEM((N_SEQ, PAIR, 2 * HD), BF16),
            pltpu.VMEM((N_SEQ, PAIR, HEADS * HD), BF16),
        ]
        + [pltpu.VMEM((4, 2, 4, rows, 2 * HD), BF16) for rows in KEY_ROWS]
        + [
            pltpu.VMEM((HEADS, TOK, HD), BF16),
            pltpu.VMEM((HEADS * HD, D), BF16),
            pltpu.VMEM((HEADS * ROWS, HD), F32),
            pltpu.VMEM((HEADS * ROWS, HD), F32),
            pltpu.VMEM((HEADS * ROWS, HD), F32),
            pltpu.VMEM((ROWS, HEADS * HD), BF16),
            pltpu.VMEM((CHUNKS, N_TP, ROWS, WIDTH), BF16),
            pltpu.VMEM((CHUNKS, ROWS, WIDTH), BF16),
            pltpu.VMEM((CHUNKS, ROWS, WIDTH), BF16),
            pltpu.VMEM((CHUNKS, 2, ROWS, WIDTH), BF16),
            pltpu.VMEM((CHUNKS, 2, ROWS, WIDTH), BF16),
            pltpu.VMEM((CHUNKS, ROWS, WIDTH), BF16),
            pltpu.VMEM((CHUNKS, ROWS, WIDTH), BF16),
            pltpu.VMEM((TOK, WIDTH), F32),
            pltpu.VMEM((TOK, HD), F32),
            pltpu.VMEM((8, TOK), F32),
            pltpu.VMEM((N_TP, 8, TOK), F32),
            dma((4,)),
            dma((CHUNKS, 12)),
            dma((CHUNKS, 12)),
            dma((CHUNKS, 5)),
            dma((CHUNKS, 5)),
            dma((2,)),
            dma,
        ],
        compiler_params=pltpu.CompilerParams(
            collective_id=0, has_side_effects=True, vmem_limit_bytes=56 * 1024 * 1024
        ),
        cost_estimate=pl.CostEstimate(flops=5 * 10**9, bytes_accessed=12 * 10**6, transcendentals=5 * 10**6),
    )(
        frame_grid.reshape(2 * GRID, (HEADS + 2) * HD),
        keep_rows,
        kept_count.reshape(1, FRAMES),
        frame_slot.reshape(1, FRAMES),
        jnp.asarray(key_positions()),
        out_weight,
        residual,
        norm_gain.reshape(1, WIDTH),
    )


def solution(mesh):
    in_specs = (
        P("seq", None, "tp", None, None),
        P("seq", None),
        P(),
        P(),
        P("tp", None),
        P("seq", "tp"),
        P("tp"),
    )
    out_specs = (P("seq", "tp"), P("seq", "tp"))
    return jax.shard_map(body, mesh=mesh, in_specs=in_specs, out_specs=out_specs, check_vma=False)
```

profile of v0, /device:TPU:8, one launch (start us, length us, event | category | flops | bytes accessed | tf_op | source)
XLA Modules:
  0.0 125.4 jit_solution(8925356454327587142)
XLA Ops:
  0.6 1.3 %reshape.19.gain_ref = bf16[1,1024]{1,0:T(2,128)(2,1)} reshape(bf16[1024]{0:T(1024)(128)(2,1)} %param.14) | data formatting | bytes 4096 | tf_op jit(solution)/shard_map/reshape | solution.py:467
  1.9 1.7 %copy.13 = bf16[2,256,1,6,128]{4,3,1,0,2:T(8,128)(2,1)S(1)} copy(bf16[2,256,1,6,128]{4,1,3,2,0:T(8,128)(2,1)} %param.8) | data formatting | bytes 1572864 | tf_op jit(solution)/shard_map/reshape | solution.py:460
  3.6 1.0 copy.17
  4.6 117.0 %shard_map.95 = (bf16[256,1024]{1,0:T(8,128)(2,1)}, bf16[256,1024]{1,0:T(8,128)(2,1)}) custom-call(bf16[512,768]{1,0:T(8,128)(2,1)} %bitcast.9, s32[2,256]{1,0:T(2,128)} %keep_ref.1, s32[1,64]{1,0:T(1,128)} %bitcast.10, s32[1,64]{1,0:T(1,128)} %bitcast.11, s32[1,8192]{1,0:T(1,128)} %constant.2.clone.kpos_ref, bf16[512,8192]{1,0:T(8,128)(2,1)} %w_hbm.1, ...), custom_call_target="tpu_custom_call" | custom-call | flops 5000000000 | bytes 12000000 | tf_op jit(solution)/shard_map/pallas_call | solution.py:417
  121.6 1.9 %copy.20 = bf16[256,1024]{1,0:T(8,128)(2,1)} copy(bf16[256,1024]{1,0:T(8,128)(2,1)} %get-tuple-element.4) | data formatting | bytes 1048576
  123.5 1.9 %copy.21 = bf16[256,1024]{1,0:T(8,128)(2,1)} copy(bf16[256,1024]{1,0:T(8,128)(2,1)} %get-tuple-element.5) | data formatting | bytes 1048576
where the time goes:
time: 126 us; the launch traced here: 125 us
  Pallas kernels  117 us (93%)
  local copies, waits for them, and re-layouts  7.7 us (6%)
    pallas_call x1, Pallas kernels, body(): pl.pallas_call(kernel, out_shape=[jax.ShapeDtypeStruct((TOK, WIDTH), BF16...  117 us
    unnamed x3, local copies, waits for them, and re-layouts  4.75 us

commit v1 on v0

v1 whole, which is shorter than its diff:
```python
import math

import jax
import jax.numpy as jnp
from jax import lax
from jax.experimental import pallas as pl
from jax.experimental.pallas import tpu as pltpu
from jax.sharding import PartitionSpec as P

D = 8192
HD = 128
HEADS = 4
FRAMES = 64
GRID = 256
TOK = 256
N_SEQ = 32
N_TP = 8
WIDTH = D // N_TP
PAIR = 16
QUERY_AT = (0, 64, 128, 192, 256)
KEY_AT = (0, 80, 144, 208, 256)
CHUNKS = 4
KEY_ROWS = tuple(KEY_AT[i + 1] - KEY_AT[i] for i in range(CHUNKS))
KEY_BLOCKS = (1, 1, 1, 1)
MOST = max(QUERY_AT[i + 1] - QUERY_AT[i] for i in range(CHUNKS))
UNIT = 32
UNITS = TOK // UNIT
PAIR_FIRST = (False, True, False, True, False, True, False, True)
UNITS_OF = ((0, 1), (2, 3), (4, 5), (6, 7))
X_DIRECT = False
NEGATIVE = -1e30
FAR = 1 << 20
EPSILON = 1e-06
SCALE = math.log2(math.e) / math.sqrt(HD)
MESH = pl.DeviceIdType.MESH
F32 = jnp.float32
BF16 = jnp.bfloat16


def iota(shape, dim):
    return lax.broadcasted_iota(jnp.int32, shape, dim)


def one_hot(mask):
    return jnp.where(mask, 1.0, 0.0).astype(BF16)


def dot(a, b, contract):
    return lax.dot_general(a, b, ((contract[:1], contract[1:]), ((), ())), preferred_element_type=F32)


def kernel(
    x_ref, keep_ref, count_ref, slot_ref, w_hbm, res_ref,
    stream_ref, inverse_ref,
    send_kv, send_q, recv_kv, recv_q, kv0, kv1, kv2, kv3, seen0, seen1, seen2, seen3, q_ref, bias_ref, w_ref,
    m_ref, acc_ref, att_ref, part_ref, pair_ref, half_send, half_p, half_m, near_send, block_p, block_m,
    z_send, z_recv, ssq_ref, ssq_send, ssq_recv,
    a2a_sem, g_send, g_recv, r_send, r_recv, s_sem, w_sem,
):
    kvs, seen = (kv0, kv1, kv2, kv3), (seen0, seen1, seen2, seen3)
    me = lax.axis_index("seq")
    tp = lax.axis_index("tp")
    zz, xx, cc = me >> 3, (me >> 1) & 3, me & 1
    yy, zl = tp >> 1, tp & 1
    y_up, y_down, y_far = (yy + 1) & 3, (yy - 1) & 3, (yy + 2) & 3

    def seq_id(z, x, c):
        return {"seq": (((z & 3) * 4 + (x & 3)) * 2 + c)}

    def tp_id(y, z):
        return {"tp": (y & 3) * 2 + z}

    to_send, to_recv = {}, {}

    def start(copies):
        for key, copy in copies:
            copy.start()
            to_send[key] = to_recv[key] = copy

    def wait_recv(copies):
        for key, copy in copies:
            copy.wait_recv()
            to_recv.pop(key)

    w_copy = pltpu.make_async_copy(w_hbm, w_ref, w_sem)
    w_copy.start()

    barrier = pltpu.get_barrier_semaphore()

    @pl.loop(1, N_SEQ)
    def _(o):
        pl.semaphore_signal(barrier, inc=1, device_id={"seq": (me + o) & 31}, device_id_type=MESH)

    @pl.loop(1, N_TP)
    def _(o):
        pl.semaphore_signal(barrier, inc=1, device_id={"tp": (tp + o) & 7}, device_id_type=MESH)

    f_col, f_row = iota((FRAMES, FRAMES), 0), iota((FRAMES, FRAMES), 1)
    counts, slots = count_ref[...], slot_ref[...]
    starts_col = jnp.sum(jnp.where(f_row < f_col, counts, 0), axis=1, keepdims=True)
    count_col = jnp.sum(jnp.where(f_row == f_col, counts, 0), axis=1, keepdims=True)
    slot_col = jnp.sum(jnp.where(f_row == f_col, slots, 0), axis=1, keepdims=True)

    r_id = iota((N_SEQ * PAIR, 1), 0)
    second = ((r_id >> 3) & 1) == 1

    def own(fl, values):
        return jnp.sum(jnp.where(slot_col == 2 * me + fl, values, 0), axis=0, keepdims=True)

    first_r = jnp.where(second, own(1, starts_col), own(0, starts_col))
    count_r = jnp.where(second, own(1, count_col), own(0, count_col))
    offset_r = (((r_id >> 4) - first_r) & 31) + 32 * (r_id & 7)
    offset_r = jnp.where(offset_r < count_r, offset_r, -1)
    picked = []
    for fl in range(2):
        wanted = jnp.where(second if fl else jnp.logical_not(second), offset_r, -1)
        chosen = one_hot(iota((N_SEQ * PAIR, GRID), 1) == wanted)
        kept = one_hot(iota((GRID, GRID), 0) == keep_ref[fl : fl + 1, :])
        picked.append(dot(chosen, kept, (1, 1)).astype(BF16))
    pick = jnp.concatenate(picked, axis=1)

    def pick_heads(low, high):
        rows = [jnp.concatenate([x_ref[0, h], x_ref[1, h]], axis=0) for h in range(low, high)]
        return dot(pick, jnp.concatenate(rows, axis=1), (1, 0)).astype(BF16).reshape(N_SEQ, PAIR, -1)

    send_kv[...] = pick_heads(HEADS, HEADS + 2)

    pl.semaphore_wait(barrier, N_SEQ - 1 + N_TP - 1)

    def exchange(src, dst, at):
        @pl.loop(1, N_SEQ)
        def _(o):
            other = (me + o) & 31
            pltpu.make_async_remote_copy(
                src_ref=src.at[other],
                dst_ref=dst.at[me],
                send_sem=a2a_sem.at[at],
                recv_sem=a2a_sem.at[at + 1],
                device_id={"seq": other},
                device_id_type=MESH,
            ).start()

        key, copy = exchange_all(src, dst, at)[0]
        to_send[key] = to_recv[key] = copy

    def exchange_all(src, dst, at):
        copy = pltpu.make_async_remote_copy(
            src_ref=src.at[pl.ds(0, N_SEQ - 1)],
            dst_ref=dst.at[pl.ds(0, N_SEQ - 1)],
            send_sem=a2a_sem.at[at],
            recv_sem=a2a_sem.at[at + 1],
            device_id={"seq": (me + 1) & 31},
            device_id_type=MESH,
        )
        return [((2, 0, at), copy)]

    exchange(send_kv, recv_kv, 0)
    recv_kv[pl.ds(me, 1)] = send_kv[pl.ds(me, 1)]
    send_q[...] = pick_heads(0, HEADS)
    recv_q[pl.ds(me, 1)] = send_q[pl.ds(me, 1)]

    lane = iota((1, N_SEQ * PAIR), 1)
    at_slot = slot_col == (iota((FRAMES, N_SEQ * PAIR), 1) >> 3)
    first_l = jnp.sum(jnp.where(at_slot, starts_col, 0), axis=0, keepdims=True)
    count_l = jnp.sum(jnp.where(at_slot, count_col, 0), axis=0, keepdims=True)
    offset_l = ((me - first_l) & 31) + 32 * (lane & 7)
    row_l = jnp.where(offset_l < count_l, (first_l + offset_l) >> 5, -1)
    place = one_hot(iota((TOK, N_SEQ * PAIR), 0) == row_l)

    wait_recv(exchange_all(send_kv, recv_kv, 0))
    mine = dot(place, recv_kv[...].reshape(N_SEQ * PAIR, 2 * HD), (1, 0)).astype(BF16)
    for c in range(CHUNKS):
        kvs[c][xx, cc, zz] = mine[KEY_AT[c] : KEY_AT[c + 1], :]

    def seq_copy(c, at, src, dst, device):
        return (0, c, at), pltpu.make_async_remote_copy(
            src_ref=src, dst_ref=dst, send_sem=g_send.at[c, at], recv_sem=g_recv.at[c, at],
            device_id=device, device_id_type=MESH,
        )

    def z_all(c):
        ref = kvs[c].at[xx, cc, zz]
        return [seq_copy(c, step, ref, ref, seq_id(zz + step + 1, xx, cc)) for step in range(3)]

    def x_one(c):
        ref = kvs[c].at[xx, cc]
        steps = (1, 2, 3) if X_DIRECT else (1, 3)
        return [seq_copy(c, 2 + step, ref, ref, seq_id(zz, xx + step, cc)) for step in steps]

    def x_two(c):
        up = kvs[c].at[(xx - 1) & 3, cc, pl.ds(0, 2)]
        down = kvs[c].at[(xx + 1) & 3, cc, pl.ds(2, 2)]
        return [
            seq_copy(c, 6, up, up, seq_id(zz, xx + 1, cc)),
            seq_copy(c, 7, down, down, seq_id(zz, xx - 1, cc)),
        ]

    def sibling(c, step):
        ref = kvs[c].at[(xx + step) & 3, cc]
        return [seq_copy(c, 8 + step, ref, ref, seq_id(zz, xx, 1 - cc))]

    def gather_stage(stage, c):
        if stage == 0:
            start(z_all(c))
        elif stage == 1:
            wait_recv(z_all(c))
            start(x_one(c))
            start(sibling(c, 0))
        elif stage == 2:
            wait_recv(x_one(c))
            if not X_DIRECT:
                start(x_two(c))
            for step in (1, 3, 2) if X_DIRECT else (1, 3):
                start(sibling(c, step))
        elif stage == 3:
            if not X_DIRECT:
                wait_recv(x_two(c))
                start(sibling(c, 2))
        elif stage == 4:
            for step in range(4):
                wait_recv(sibling(c, step))

    def mark_keys():
        lanes = iota((1, HD), 1)
        firsts = jnp.sum(jnp.where(iota((FRAMES, HD), 0) < lanes, count_col, 0), axis=0, keepdims=True)
        firsts = jnp.where(lanes < FRAMES, firsts, FAR)
        q_pos = iota((TOK, 1), 0) * N_SEQ + me
        ends = jnp.min(jnp.where(firsts > q_pos, firsts, FAR), axis=1, keepdims=True)
        bias_ref[...] = jnp.where((firsts == ends) & (firsts < FAR), NEGATIVE, 0.0).astype(BF16)
        for c in range(CHUNKS):
            rows = KEY_ROWS[c]

            @pl.loop(0, N_SEQ)
            def _(i, c=c, rows=rows):
                x, core, z = i >> 3, (i >> 2) & 1, i & 3
                pos = (KEY_AT[c] + iota((rows, 1), 0)) * N_SEQ + (z * 4 + x) * 2 + core
                seen[c][pl.ds(pl.multiple_of(i * rows, 16), rows), :] = one_hot(pos >= firsts)

    def load_queries():
        wait_recv(exchange_all(send_q, recv_q, 2))
        queries = dot(place, recv_q[...].reshape(N_SEQ * PAIR, HEADS * HD), (1, 0)).astype(BF16)
        for a in range(HEADS):
            q_ref[a] = queries[:, a * HD : (a + 1) * HD]

    def attention(j, parts):
        low, high = QUERY_AT[j], QUERY_AT[j + 1]
        rows = HEADS * (high - low)
        q = jnp.concatenate(
            [q_ref[:, low:high, :].reshape(rows, HD), jnp.concatenate([bias_ref[low:high, :]] * HEADS, axis=0)], axis=1
        )
        if 0 in parts:
            m_ref[:rows] = jnp.full((rows, HD), NEGATIVE, F32)
            acc_ref[:rows] = jnp.zeros((rows, 2 * HD), F32)
        for c in parts:
            block = KEY_ROWS[c] * N_SEQ // KEY_BLOCKS[c]
            flat = kvs[c].reshape(KEY_ROWS[c] * N_SEQ, 2 * HD)

            def step(i, c=c, block=block, flat=flat):
                at = pl.multiple_of(i * block, 128)
                keys = jnp.concatenate([flat[pl.ds(at, block), :HD], seen[c][pl.ds(at, block), :]], axis=1)
                values = jnp.concatenate([flat[pl.ds(at, block), HD:], jnp.ones((block, HD), BF16)], axis=1)
                s = dot(q, keys, (1, 1))
                old = m_ref[:rows, :1]
                new = jnp.maximum(old, jnp.max(s, axis=1, keepdims=True))
                p = jnp.exp2((s - new) * SCALE).astype(BF16)
                keep = jnp.exp2((old - new) * SCALE)
                m_ref[:rows] = jnp.broadcast_to(new, (rows, HD))
                acc_ref[:rows] = acc_ref[:rows] * keep + dot(p, values, (1, 0))

            if KEY_BLOCKS[c] == 1:
                step(0)
            else:
                pl.loop(0, KEY_BLOCKS[c])(step)

        if j in parts:
            out = (acc_ref[:rows, :HD] / acc_ref[:rows, HD:]).astype(BF16)
            wide = [out[a * (high - low) : (a + 1) * (high - low)] for a in range(HEADS)]
            att_ref[: high - low] = jnp.concatenate(wide, axis=1)

    def tp_copy(u, at, src, dst, device):
        return (1, u, at), pltpu.make_async_remote_copy(
            src_ref=src, dst_ref=dst, send_sem=r_send.at[u, at], recv_sem=r_recv.at[u, at],
            device_id=device, device_id_type=MESH,
        )

    def far_halves(u):
        if PAIR_FIRST[u]:
            columns = pl.ds(0, WIDTH // 2)
            return [
                tp_copy(u, 0, half_send.at[u, 0], half_p.at[u, :, columns], tp_id(yy + 1, zl)),
                tp_copy(u, 1, half_send.at[u, 1], half_m.at[u, :, columns], tp_id(yy - 1, zl)),
            ]
        return [
            tp_copy(u, 0, part_ref.at[u, 0, y_far], half_p.at[u], tp_id(yy + 1, zl)),
            tp_copy(u, 1, part_ref.at[u, 1, y_far], half_m.at[u], tp_id(yy - 1, zl)),
        ]

    def near_blocks(u):
        if PAIR_FIRST[u]:
            return [
                tp_copy(u, 2, near_send.at[u, 0], block_p.at[u, 0], tp_id(yy + 1, zl)),
                tp_copy(u, 3, near_send.at[u, 1], block_m.at[u, 0], tp_id(yy - 1, zl)),
            ]
        return [
            tp_copy(u, 2, part_ref.at[u, :, y_up], block_p.at[u], tp_id(yy + 1, zl)),
            tp_copy(u, 3, part_ref.at[u, :, y_down], block_m.at[u], tp_id(yy - 1, zl)),
        ]

    def z_pair(u):
        return [tp_copy(u, 4, z_send.at[u], z_recv.at[u], tp_id(yy, 1 - zl))]

    def z_piece(u, step):
        y = (yy + step) & 3
        return [tp_copy(u, 4 + step, part_ref.at[u, 1 - zl, y], pair_ref.at[u, y], tp_id(yy, 1 - zl))]

    def project(j):
        low, high = QUERY_AT[j], QUERY_AT[j + 1]
        for step in (2, 1, 3, 0):
            y = (yy + step) & 3
            w = w_ref[:, pl.ds(pl.multiple_of(y * 2 * WIDTH, 2 * WIDTH), 2 * WIDTH)]
            out = dot(att_ref[: high - low], w, (1, 0)).astype(BF16)
            for n, u in enumerate(UNITS_OF[j]):
                part_ref[u, 0, y] = out[n * UNIT : (n + 1) * UNIT, :WIDTH]
                part_ref[u, 1, y] = out[n * UNIT : (n + 1) * UNIT, WIDTH:]
            for u in UNITS_OF[j]:
                if PAIR_FIRST[u]:
                    start(z_piece(u, step))
                elif step == 2:
                    start(far_halves(u))

    def paired(u, y):
        return part_ref[u, zl, y].astype(F32) + pair_ref[u, y].astype(F32)

    def reduce_pair(u):
        wait_recv(z_piece(u, 2))
        both = paired(u, y_far).astype(BF16)
        half_send[u, 0] = both[:, : WIDTH // 2]
        half_send[u, 1] = both[:, WIDTH // 2 :]
        start(far_halves(u))

    def reduce_near(u):
        if PAIR_FIRST[u]:
            half = WIDTH // 2
            wait_recv(z_piece(u, 1) + z_piece(u, 3) + far_halves(u))
            up, down = paired(u, y_up), paired(u, y_down)
            near_send[u, 0, :, :half] = (up[:, :half] + half_p[u, :, :half].astype(F32)).astype(BF16)
            near_send[u, 0, :, half:] = up[:, half:].astype(BF16)
            near_send[u, 1, :, :half] = down[:, :half].astype(BF16)
            near_send[u, 1, :, half:] = (down[:, half:] + half_m[u, :, :half].astype(F32)).astype(BF16)
        else:
            wait_recv(far_halves(u))
            part_ref[u, 0, y_up] = (part_ref[u, 0, y_up].astype(F32) + half_p[u].astype(F32)).astype(BF16)
            part_ref[u, 1, y_down] = (part_ref[u, 1, y_down].astype(F32) + half_m[u].astype(F32)).astype(BF16)
        start(near_blocks(u))

    def reduce_own(u):
        wait_recv(near_blocks(u))
        rows = pl.ds(u * UNIT, UNIT)

        def total(h):
            return part_ref[u, h, yy].astype(F32) + block_p[u, h].astype(F32) + block_m[u, h].astype(F32)

        if PAIR_FIRST[u]:
            wait_recv(z_piece(u, 0))
            finish(rows, paired(u, yy) + block_p[u, 0].astype(F32) + block_m[u, 0].astype(F32) + res_ref[rows, :].astype(F32))
        else:
            z_send[u] = total(1 - zl).astype(BF16)
            start(z_pair(u))
            stream_ref[rows, :] = total(zl) + res_ref[rows, :].astype(F32)

    def finish(rows, stream):
        stream_ref[rows, :] = stream
        ssq_ref[rows, :] = jnp.broadcast_to(jnp.sum(stream * stream, axis=1, keepdims=True), (UNIT, HD))

    def finish_rows(u):
        if not PAIR_FIRST[u]:
            wait_recv(z_pair(u))
            rows = pl.ds(u * UNIT, UNIT)
            finish(rows, stream_ref[rows, :] + z_recv[u].astype(F32))

    gather_stage(0, 0)
    gather_stage(0, 1)
    gather_stage(0, 2)
    gather_stage(0, 3)
    gather_stage(1, 0)
    gather_stage(1, 1)
    exchange(send_q, recv_q, 2)
    mark_keys()
    gather_stage(1, 2)
    gather_stage(1, 3)
    gather_stage(2, 0)
    gather_stage(2, 1)
    gather_stage(2, 2)
    gather_stage(2, 3)
    gather_stage(3, 0)
    gather_stage(3, 1)
    gather_stage(3, 2)
    gather_stage(3, 3)
    load_queries()
    gather_stage(4, 0)
    attention(0, (0,))
    w_copy.wait()
    project(0)
    gather_stage(4, 1)
    attention(1, (0, 1))
    reduce_pair(1)
    reduce_near(0)
    project(1)
    gather_stage(4, 2)
    attention(2, (0, 1, 2))
    reduce_pair(3)
    reduce_near(2)
    reduce_near(1)
    reduce_own(0)
    project(2)
    gather_stage(4, 3)
    attention(3, (0, 1, 2, 3))
    reduce_pair(5)
    reduce_near(4)
    reduce_near(3)
    reduce_own(2)
    reduce_own(1)
    finish_rows(0)
    project(3)
    reduce_pair(7)
    reduce_near(6)
    reduce_near(5)
    reduce_own(4)
    reduce_own(3)
    finish_rows(2)
    reduce_near(7)
    reduce_own(6)
    reduce_own(5)
    finish_rows(4)
    reduce_own(7)
    finish_rows(6)

    diag = iota((TOK, TOK), 0) == iota((TOK, TOK), 1)
    ssq_row = jnp.sum(jnp.where(diag, ssq_ref[:, :1], 0.0), axis=0, keepdims=True)
    ssq_send[...] = jnp.broadcast_to(ssq_row, (8, TOK))
    ssq_recv[pl.ds(tp, 1)] = ssq_send[...][None]

    @pl.loop(1, N_TP)
    def _(o):
        pltpu.make_async_remote_copy(
            src_ref=ssq_send, dst_ref=ssq_recv.at[tp], send_sem=s_sem.at[0], recv_sem=s_sem.at[1],
            device_id={"tp": (tp + o) & 7}, device_id_type=MESH,
        ).start()

    ssq_all = pltpu.make_async_remote_copy(
        src_ref=ssq_recv.at[pl.ds(0, N_TP - 1)], dst_ref=ssq_recv.at[pl.ds(0, N_TP - 1)],
        send_sem=s_sem.at[0], recv_sem=s_sem.at[1],
        device_id={"tp": (tp + 1) & 7}, device_id_type=MESH,
    )
    for key in to_send:
        to_send[key].wait_send()
    ssq_all.wait_recv()
    sums = jnp.sum(ssq_recv[...], axis=0)[:1, :]
    inverse_row = lax.rsqrt(sums / D + EPSILON)
    inverse = jnp.sum(jnp.where(diag, inverse_row, 0.0), axis=1, keepdims=True)
    inverse_ref[...] = jnp.broadcast_to(inverse, (TOK, HD))
    ssq_all.wait_send()


def normalize(stream_ref, inverse_ref, gain_ref, hid_ref, nrm_ref):
    stream = stream_ref[...]
    gain = gain_ref[...].astype(F32).reshape(1, WIDTH)
    hid_ref[...] = stream.astype(BF16)
    nrm_ref[...] = (stream * inverse_ref[:, :1] * gain).astype(BF16)


def body(frame_grid, keep_rows, kept_count, frame_slot, out_weight, residual, norm_gain):
    vmem = pl.BlockSpec(memory_space=pltpu.VMEM)
    dma = pltpu.SemaphoreType.DMA
    stream, inverse = pl.pallas_call(
        kernel,
        out_shape=[jax.ShapeDtypeStruct((TOK, WIDTH), F32), jax.ShapeDtypeStruct((TOK, HD), F32)],
        in_specs=[vmem] * 4 + [pl.BlockSpec(memory_space=pl.ANY)] + [vmem],
        out_specs=[vmem] * 2,
        scratch_shapes=[
            pltpu.VMEM((N_SEQ, PAIR, 2 * HD), BF16),
            pltpu.VMEM((N_SEQ, PAIR, HEADS * HD), BF16),
            pltpu.VMEM((N_SEQ, PAIR, 2 * HD), BF16),
            pltpu.VMEM((N_SEQ, PAIR, HEADS * HD), BF16),
        ]
        + [pltpu.VMEM((4, 2, 4, rows, 2 * HD), BF16) for rows in KEY_ROWS]
        + [pltpu.VMEM((N_SEQ * rows, HD), BF16) for rows in KEY_ROWS]
        + [
            pltpu.VMEM((HEADS, TOK, HD), BF16),
            pltpu.VMEM((TOK, HD), BF16),
            pltpu.VMEM((HEADS * HD, D), BF16),
            pltpu.VMEM((HEADS * MOST, HD), F32),
            pltpu.VMEM((HEADS * MOST, 2 * HD), F32),
            pltpu.VMEM((MOST, HEADS * HD), BF16),
            pltpu.VMEM((UNITS, 2, 4, UNIT, WIDTH), BF16),
            pltpu.VMEM((UNITS, 4, UNIT, WIDTH), BF16),
            pltpu.VMEM((UNITS, 2, UNIT, WIDTH // 2), BF16),
            pltpu.VMEM((UNITS, UNIT, WIDTH), BF16),
            pltpu.VMEM((UNITS, UNIT, WIDTH), BF16),
            pltpu.VMEM((UNITS, 2, UNIT, WIDTH), BF16),
            pltpu.VMEM((UNITS, 2, UNIT, WIDTH), BF16),
            pltpu.VMEM((UNITS, 2, UNIT, WIDTH), BF16),
            pltpu.VMEM((UNITS, UNIT, WIDTH), BF16),
            pltpu.VMEM((UNITS, UNIT, WIDTH), BF16),
            pltpu.VMEM((TOK, HD), F32),
            pltpu.VMEM((8, TOK), F32),
            pltpu.VMEM((N_TP, 8, TOK), F32),
            dma((4,)),
            dma((CHUNKS, 12)),
            dma((CHUNKS, 12)),
            dma((UNITS, 8)),
            dma((UNITS, 8)),
            dma((2,)),
            dma,
        ],
        compiler_params=pltpu.CompilerParams(
            collective_id=0, has_side_effects=True, vmem_limit_bytes=56 * 1024 * 1024
        ),
        cost_estimate=pl.CostEstimate(flops=5 * 10**9, bytes_accessed=12 * 10**6, transcendentals=5 * 10**6),
    )(
        frame_grid[:, :, 0].transpose(0, 2, 1, 3),
        keep_rows,
        kept_count.reshape(1, FRAMES),
        frame_slot.reshape(1, FRAMES),
        out_weight,
        residual,
    )
    return pl.pallas_call(
        normalize,
        out_shape=[jax.ShapeDtypeStruct((TOK, WIDTH), BF16)] * 2,
        in_specs=[vmem] * 3,
        out_specs=[vmem] * 2,
        cost_estimate=pl.CostEstimate(flops=10**6, bytes_accessed=2 * 10**6, transcendentals=0),
    )(stream, inverse, norm_gain)


def solution(mesh):
    in_specs = (
        P("seq", None, "tp", None, None),
        P("seq", None),
        P(),
        P(),
        P("tp", None),
        P("seq", "tp"),
        P("tp"),
    )
    out_specs = (P("seq", "tp"), P("seq", "tp"))
    return jax.shard_map(body, mesh=mesh, in_specs=in_specs, out_specs=out_specs, check_vma=False)
```

time: 126 us -> 101 us (0.80)
  Pallas kernels: 117 us -> 101 us
  local copies, waits for them, and re-layouts: 7.7 us -> 0 us
    pallas_call x1 -> x2, Pallas kernels: 117 us -> 101 us  [the longest x1 98.1 us: body(): pl.pallas_call(kernel, out_shape=[jax.ShapeDtypeStruct((TOK, WIDTH), F32)...]
    unnamed x3 -> x0, local copies, waits for them, and re-layouts: 4.75 us -> none
    reshape x2 -> x0, local copies, waits for them, and re-layouts: 2.95 us -> none  [the longest x1 1.68 us: body(): frame_grid.reshape(2 * GRID, (HEADS + 2) * HD)]
where the time goes in v1:
time: 101 us
  Pallas kernels  101 us (100%)
    pallas_call x1, Pallas kernels, body(): pl.pallas_call(kernel, out_shape=[jax.ShapeDtypeStruct((TOK, WIDTH), F32)...  98.1 us
    pallas_call x1, Pallas kernels, body(): pl.pallas_call(normalize, out_shape=[jax.ShapeDtypeStruct((TOK, WIDTH), B...  2.43 us

profile of v1, /device:TPU:8, one launch (start us, length us, event | category | flops | bytes accessed | tf_op | source)
XLA Modules:
  0.0 101.2 jit_solution(5123615674826955450)
XLA Ops:
  0.6 98.1 %shard_map.86 = (f32[256,1024]{1,0:T(8,128)}, f32[256,128]{1,0:T(8,128)}) custom-call(bf16[2,6,256,128]{3,2,1,0:T(8,128)(2,1)} %bitcast.5, s32[2,256]{1,0:T(2,128)} %keep_ref.1, s32[1,64]{1,0:T(1,128)} %bitcast.6, s32[1,64]{1,0:T(1,128)} %bitcast.7, bf16[512,8192]{1,0:T(8,128)(2,1)} %w_hbm.1, bf16[256,1024]{1,0:T(8,128)(2,1)} %res_ref.1), custom_call_target="tpu_custom_call" | custom-call | flops 5000000000 | bytes 12000000 | tf_op jit(solution)/shard_map/pallas_call | solution.py:475
  98.8 2.4 %shard_map.87 = (bf16[256,1024]{1,0:T(8,128)(2,1)}, bf16[256,1024]{1,0:T(8,128)(2,1)}) custom-call(f32[256,1024]{1,0:T(8,128)} %get-tuple-element.4.stream_ref, f32[256,128]{1,0:T(8,128)} %get-tuple-element.5.inverse_ref, bf16[1024]{0:T(1024)(128)(2,1)} %gain_ref.1), custom_call_target="tpu_custom_call" | custom-call | flops 1000000 | bytes 2000000 | tf_op jit(solution)/shard_map/pallas_call | solution.py:528

commit v2 on v1

--- a/solution.py
+++ b/solution.py
@@ -379,59 +379,59 @@
             finish(rows, stream_ref[rows, :] + z_recv[u].astype(F32))
 
     gather_stage(0, 0)
+    gather_stage(0, 2)
     gather_stage(0, 1)
-    gather_stage(0, 2)
+    gather_stage(1, 0)
+    exchange(send_q, recv_q, 2)
+    gather_stage(1, 2)
+    mark_keys()
+    gather_stage(2, 0)
+    gather_stage(1, 1)
+    gather_stage(2, 2)
     gather_stage(0, 3)
-    gather_stage(1, 0)
-    gather_stage(1, 1)
-    exchange(send_q, recv_q, 2)
-    mark_keys()
-    gather_stage(1, 2)
-    gather_stage(1, 3)
-    gather_stage(2, 0)
-    gather_stage(2, 1)
-    gather_stage(2, 2)
-    gather_stage(2, 3)
     gather_stage(3, 0)
-    gather_stage(3, 1)
-    gather_stage(3, 2)
-    gather_stage(3, 3)
     load_queries()
     gather_stage(4, 0)
     attention(0, (0,))
+    gather_stage(2, 1)
     w_copy.wait()
     project(0)
+    gather_stage(3, 2)
+    gather_stage(1, 3)
+    gather_stage(3, 1)
+    gather_stage(4, 2)
+    reduce_near(0)
     gather_stage(4, 1)
+    reduce_pair(1)
     attention(1, (0, 1))
-    reduce_pair(1)
-    reduce_near(0)
+    gather_stage(2, 3)
     project(1)
-    gather_stage(4, 2)
     attention(2, (0, 1, 2))
-    reduce_pair(3)
-    reduce_near(2)
+    gather_stage(3, 3)
     reduce_near(1)
     reduce_own(0)
     project(2)
     gather_stage(4, 3)
+    reduce_near(2)
+    reduce_pair(3)
     attention(3, (0, 1, 2, 3))
-    reduce_pair(5)
     reduce_near(4)
-    reduce_near(3)
-    reduce_own(2)
     reduce_own(1)
     finish_rows(0)
     project(3)
+    reduce_pair(5)
+    reduce_own(2)
+    reduce_near(3)
+    reduce_own(4)
     reduce_pair(7)
     reduce_near(6)
     reduce_near(5)
-    reduce_own(4)
     reduce_own(3)
+    reduce_near(7)
     finish_rows(2)
-    reduce_near(7)
     reduce_own(6)
+    finish_rows(4)
     reduce_own(5)
-    finish_rows(4)
     reduce_own(7)
     finish_rows(6)
 

time: 101 us -> 95.6 us (0.947)
  Pallas kernels: 101 us -> 94.6 us
    pallas_call x1, Pallas kernels: 98.1 us -> 92.1 us  [body(): pl.pallas_call(kernel, out_shape=[jax.ShapeDtypeStruct((TOK, WIDTH), F32)...]
where the time goes in v2:
time: 95.6 us; the launch traced here: 95.2 us
  Pallas kernels  94.6 us (99%)
    pallas_call x1, Pallas kernels, body(): pl.pallas_call(kernel, out_shape=[jax.ShapeDtypeStruct((TOK, WIDTH), F32)...  92.1 us
    pallas_call x1, Pallas kernels, body(): pl.pallas_call(normalize, out_shape=[jax.ShapeDtypeStruct((TOK, WIDTH), B...  2.43 us

profile of v2, /device:TPU:8, one launch (start us, length us, event | category | flops | bytes accessed | tf_op | source)
XLA Modules:
  0.0 95.2 jit_solution(8905956155173749382)
XLA Ops:
  0.6 92.1 %shard_map.86 = (f32[256,1024]{1,0:T(8,128)}, f32[256,128]{1,0:T(8,128)}) custom-call(bf16[2,6,256,128]{3,2,1,0:T(8,128)(2,1)} %bitcast.5, s32[2,256]{1,0:T(2,128)} %keep_ref.1, s32[1,64]{1,0:T(1,128)} %bitcast.6, s32[1,64]{1,0:T(1,128)} %bitcast.7, bf16[512,8192]{1,0:T(8,128)(2,1)} %w_hbm.1, bf16[256,1024]{1,0:T(8,128)(2,1)} %res_ref.1), custom_call_target="tpu_custom_call" | custom-call | flops 5000000000 | bytes 12000000 | tf_op jit(solution)/shard_map/pallas_call | solution.py:475
  92.8 2.4 %shard_map.87 = (bf16[256,1024]{1,0:T(8,128)(2,1)}, bf16[256,1024]{1,0:T(8,128)(2,1)}) custom-call(f32[256,1024]{1,0:T(8,128)} %get-tuple-element.4.stream_ref, f32[256,128]{1,0:T(8,128)} %get-tuple-element.5.inverse_ref, bf16[1024]{0:T(1024)(128)(2,1)} %gain_ref.1), custom_call_target="tpu_custom_call" | custom-call | flops 1000000 | bytes 2000000 | tf_op jit(solution)/shard_map/pallas_call | solution.py:528

commit v3 on v2

--- a/solution.py
+++ b/solution.py
@@ -27,7 +27,7 @@
 UNITS = TOK // UNIT
 PAIR_FIRST = (False, True, False, True, False, True, False, True)
 UNITS_OF = ((0, 1), (2, 3), (4, 5), (6, 7))
-X_DIRECT = False
+Z_DIRECT = (0, 1, 2, 3)
 NEGATIVE = -1e30
 FAR = 1 << 20
 EPSILON = 1e-06
@@ -128,9 +128,8 @@
     pl.semaphore_wait(barrier, N_SEQ - 1 + N_TP - 1)
 
     def exchange(src, dst, at):
-        @pl.loop(1, N_SEQ)
-        def _(o):
-            other = (me + o) & 31
+        def send(z, low):
+            other = ((zz + z) & 3) * 8 + ((me + low) & 7)
             pltpu.make_async_remote_copy(
                 src_ref=src.at[other],
                 dst_ref=dst.at[me],
@@ -139,6 +138,17 @@
                 device_id={"seq": other},
                 device_id_type=MESH,
             ).start()
+
+        @pl.loop(0, 7)
+        def _(i):
+            send(2, i)
+            send(1, i)
+            send(3, i)
+            send(0, i + 1)
+
+        send(2, 7)
+        send(1, 7)
+        send(3, 7)
 
         key, copy = exchange_all(src, dst, at)[0]
         to_send[key] = to_recv[key] = copy
@@ -178,14 +188,29 @@
             device_id=device, device_id_type=MESH,
         )
 
-    def z_all(c):
+    def z_one(c):
         ref = kvs[c].at[xx, cc, zz]
-        return [seq_copy(c, step, ref, ref, seq_id(zz + step + 1, xx, cc)) for step in range(3)]
+        steps = (0, 1, 2) if c in Z_DIRECT else (0, 2)
+        return [seq_copy(c, step, ref, ref, seq_id(zz + step + 1, xx, cc)) for step in steps]
+
+    def z_two(c):
+        if c in Z_DIRECT:
+            return []
+        cut = KEY_ROWS[c] // 32 * 16
+        up = kvs[c].at[xx, cc, (zz - 1) & 3, pl.ds(0, cut)]
+        down = kvs[c].at[xx, cc, (zz + 1) & 3, pl.ds(cut, KEY_ROWS[c] - cut)]
+        return [
+            seq_copy(c, 1, up, up, seq_id(zz + 1, xx, cc)),
+            seq_copy(c, 4, down, down, seq_id(zz - 1, xx, cc)),
+        ]
+
+    def gather_z(c):
+        wait_recv(z_one(c))
+        start(z_two(c))
 
     def x_one(c):
         ref = kvs[c].at[xx, cc]
-        steps = (1, 2, 3) if X_DIRECT else (1, 3)
-        return [seq_copy(c, 2 + step, ref, ref, seq_id(zz, xx + step, cc)) for step in steps]
+        return [seq_copy(c, 2 + step, ref, ref, seq_id(zz, xx + step, cc)) for step in (1, 3)]
 
     def x_two(c):
         up = kvs[c].at[(xx - 1) & 3, cc, pl.ds(0, 2)]
@@ -201,21 +226,19 @@
 
     def gather_stage(stage, c):
         if stage == 0:
-            start(z_all(c))
+            start(z_one(c))
         elif stage == 1:
-            wait_recv(z_all(c))
+            wait_recv(z_one(c) if c in Z_DIRECT else z_two(c))
             start(x_one(c))
             start(sibling(c, 0))
         elif stage == 2:
             wait_recv(x_one(c))
-            if not X_DIRECT:
-                start(x_two(c))
-            for step in (1, 3, 2) if X_DIRECT else (1, 3):
+            start(x_two(c))
+            for step in (1, 3):
                 start(sibling(c, step))
         elif stage == 3:
-            if not X_DIRECT:
-                wait_recv(x_two(c))
-                start(sibling(c, 2))
+            wait_recv(x_two(c))
+            start(sibling(c, 2))
         elif stage == 4:
             for step in range(4):
                 wait_recv(sibling(c, step))
@@ -406,10 +429,10 @@
     attention(1, (0, 1))
     gather_stage(2, 3)
     project(1)
+    reduce_near(1)
+    reduce_own(0)
     attention(2, (0, 1, 2))
     gather_stage(3, 3)
-    reduce_near(1)
-    reduce_own(0)
     project(2)
     gather_stage(4, 3)
     reduce_near(2)
@@ -440,8 +463,7 @@
     ssq_send[...] = jnp.broadcast_to(ssq_row, (8, TOK))
     ssq_recv[pl.ds(tp, 1)] = ssq_send[...][None]
 
-    @pl.loop(1, N_TP)
-    def _(o):
+    for o in (4, 3, 5, 2, 6, 1, 7):
         pltpu.make_async_remote_copy(
             src_ref=ssq_send, dst_ref=ssq_recv.at[tp], send_sem=s_sem.at[0], recv_sem=s_sem.at[1],
             device_id={"tp": (tp + o) & 7}, device_id_type=MESH,

time: 95.6 us -> 94.8 us (level)
  no operation moved by 1% of the time
where the time goes in v3:
time: 94.8 us; the launch traced here: 94.7 us
  Pallas kernels  94.1 us (99%)
    pallas_call x1, Pallas kernels, body(): pl.pallas_call(kernel, out_shape=[jax.ShapeDtypeStruct((TOK, WIDTH), F32)...  91.6 us
    pallas_call x1, Pallas kernels, body(): pl.pallas_call(normalize, out_shape=[jax.ShapeDtypeStruct((TOK, WIDTH), B...  2.43 us

profile of v3, /device:TPU:8, one launch (start us, length us, event | category | flops | bytes accessed | tf_op | source)
XLA Modules:
  0.0 94.7 jit_solution(6640888160033991362)
XLA Ops:
  0.6 91.6 %shard_map.86 = (f32[256,1024]{1,0:T(8,128)}, f32[256,128]{1,0:T(8,128)}) custom-call(bf16[2,6,256,128]{3,2,1,0:T(8,128)(2,1)} %bitcast.5, s32[2,256]{1,0:T(2,128)} %keep_ref.1, s32[1,64]{1,0:T(1,128)} %bitcast.6, s32[1,64]{1,0:T(1,128)} %bitcast.7, bf16[512,8192]{1,0:T(8,128)(2,1)} %w_hbm.1, bf16[256,1024]{1,0:T(8,128)(2,1)} %res_ref.1), custom_call_target="tpu_custom_call" | custom-call | flops 5000000000 | bytes 12000000 | tf_op jit(solution)/shard_map/pallas_call | solution.py:497
  92.3 2.4 %shard_map.87 = (bf16[256,1024]{1,0:T(8,128)(2,1)}, bf16[256,1024]{1,0:T(8,128)(2,1)}) custom-call(f32[256,1024]{1,0:T(8,128)} %get-tuple-element.4.stream_ref, f32[256,128]{1,0:T(8,128)} %get-tuple-element.5.inverse_ref, bf16[1024]{0:T(1024)(128)(2,1)} %gain_ref.1), custom_call_target="tpu_custom_call" | custom-call | flops 1000000 | bytes 2000000 | tf_op jit(solution)/shard_map/pallas_call | solution.py:550

commit v4 on v3

--- a/solution.py
+++ b/solution.py
@@ -87,9 +87,13 @@
 
     barrier = pltpu.get_barrier_semaphore()
 
-    @pl.loop(1, N_SEQ)
-    def _(o):
-        pl.semaphore_signal(barrier, inc=1, device_id={"seq": (me + o) & 31}, device_id_type=MESH)
+    def greet(z, low):
+        other = ((zz + z) & 3) * 8 + ((me + low) & 7)
+        pl.semaphore_signal(barrier, inc=1, device_id={"seq": other}, device_id_type=MESH)
+
+    for z in (2, 1, 3):
+        pl.loop(0, 8)(lambda i, z=z: greet(z, (i + 4) & 7))
+    pl.loop(1, 8)(lambda i: greet(0, i))
 
     @pl.loop(1, N_TP)
     def _(o):

time: 94.8 us -> 94.9 us (level)
  no operation moved by 1% of the time
where the time goes in v4:
time: 94.9 us; the launch traced here: 94.7 us
  Pallas kernels  94.1 us (99%)
    pallas_call x1, Pallas kernels, body(): pl.pallas_call(kernel, out_shape=[jax.ShapeDtypeStruct((TOK, WIDTH), F32)...  91.6 us
    pallas_call x1, Pallas kernels, body(): pl.pallas_call(normalize, out_shape=[jax.ShapeDtypeStruct((TOK, WIDTH), B...  2.43 us

profile of v4, /device:TPU:8, one launch (start us, length us, event | category | flops | bytes accessed | tf_op | source)
XLA Modules:
  0.0 94.7 jit_solution(12040147146717707053)
XLA Ops:
  0.6 91.6 %shard_map.86 = (f32[256,1024]{1,0:T(8,128)}, f32[256,128]{1,0:T(8,128)}) custom-call(bf16[2,6,256,128]{3,2,1,0:T(8,128)(2,1)} %bitcast.5, s32[2,256]{1,0:T(2,128)} %keep_ref.1, s32[1,64]{1,0:T(1,128)} %bitcast.6, s32[1,64]{1,0:T(1,128)} %bitcast.7, bf16[512,8192]{1,0:T(8,128)(2,1)} %w_hbm.1, bf16[256,1024]{1,0:T(8,128)(2,1)} %res_ref.1), custom_call_target="tpu_custom_call" | custom-call | flops 5000000000 | bytes 12000000 | tf_op jit(solution)/shard_map/pallas_call | solution.py:501
  92.3 2.4 %shard_map.87 = (bf16[256,1024]{1,0:T(8,128)(2,1)}, bf16[256,1024]{1,0:T(8,128)(2,1)}) custom-call(f32[256,1024]{1,0:T(8,128)} %get-tuple-element.4.stream_ref, f32[256,128]{1,0:T(8,128)} %get-tuple-element.5.inverse_ref, bf16[1024]{0:T(1024)(128)(2,1)} %gain_ref.1), custom_call_target="tpu_custom_call" | custom-call | flops 1000000 | bytes 2000000 | tf_op jit(solution)/shard_map/pallas_call | solution.py:554
